TPU v7x, 128 devices: a whole 4x4x4 slice. The times are simulated.
128 devices in a mesh: occ: 64 (over z, y, x), aux: 2 (over core).
Axes of the slice: x: 4, y: 4, z: 4, core: 2. Of those that a mesh axis runs over, the one named last changes fastest.
Arguments:
- ints: bfloat16 [64, 1024, 4096], P('occ', None, 'aux'), may hold values from -0.75 to 0.75
- occ_energy: float32 [64, 4], P('occ'), may hold values from -2 to -0.5
- vir_energy: float32 [64, 256], P('occ'), may hold values from 0.5 to 4
- partners: int32 [64, 2], P('occ'), may hold values from -1 to 63, as said below
Outputs:
- gamma: float32 [64, 1024, 4096], P('occ', None, 'aux')
Inputs may be any that keep to these rules, and one draw needn't show every extreme that they name: partners[I, k] is -1 or a block J with I < J <= I + 2; the entries of one row differ when not -1.
All inputs are finite; a program needn't handle non-finite values.
Results may differ from a plain program's by a relative error of at most 0.012.
Values may be sent and summed in bfloat16 or wider, within the bound.
A program may use at most 128 MiB of HBM per device.

v0:
```python
import jax
import jax.numpy as jnp
from jax import lax
from jax.sharding import PartitionSpec as P

REACH = 2


def from_behind(array, axis, by):
    size = lax.axis_size(axis)
    pairs = [(i, i + by) for i in range(size) if 0 <= i + by < size]
    return lax.ppermute(array, axis, pairs)


def row_level(occ_row, vir_row):
    return (vir_row[None, :] - occ_row[:, None]).reshape(-1)


def contract_rows(left, right):
    return lax.dot_general(
        left, right, (((0,), (0,)), ((), ())), preferred_element_type=jnp.float32
    )


def contract_cols(left, right):
    return lax.dot_general(
        left, right, (((1,), (1,)), ((), ())), preferred_element_type=jnp.float32
    )


def body(ints, occ_energy, vir_energy, partners):
    blocks, rows, aux_local = ints.shape
    hops = (blocks - 1 + REACH) // blocks
    first = lax.axis_index("occ") * blocks
    pieces = [(ints, occ_energy, vir_energy)]
    for hop in range(1, hops + 1):
        pieces.append(
            (
                from_behind(ints, "occ", -hop),
                from_behind(occ_energy.astype(jnp.bfloat16), "occ", -hop).astype(occ_energy.dtype),
                from_behind(vir_energy.astype(jnp.bfloat16), "occ", -hop).astype(vir_energy.dtype),
            )
        )
    stack_ints = jnp.concatenate([piece[0] for piece in pieces], 0)
    stack_occ = jnp.concatenate([piece[1] for piece in pieces], 0)
    stack_vir = jnp.concatenate([piece[2] for piece in pieces], 0)
    stack_count = stack_ints.shape[0]
    gamma_stack = jnp.zeros((stack_count, rows, aux_local), jnp.float32)
    block_i = ints[0]
    level_i = row_level(occ_energy[0], vir_energy[0])
    for slot in range(REACH):
        target = partners[0, slot]
        live = target >= 0
        index = jnp.clip(target - first, 0, stack_count - 1)
        block_j = lax.dynamic_index_in_dim(stack_ints, index, 0, keepdims=False)
        level_j = row_level(
            lax.dynamic_index_in_dim(stack_occ, index, 0, keepdims=False),
            lax.dynamic_index_in_dim(stack_vir, index, 0, keepdims=False),
        )
        pair_full = lax.psum(contract_cols(block_i, block_j).astype(jnp.bfloat16), "aux").astype(
            jnp.float32
        )
        amplitudes = jnp.where(live, pair_full / (level_i[:, None] + level_j[None, :]), 0.0).astype(
            jnp.bfloat16
        )
        own_term = jnp.dot(amplitudes, block_j, preferred_element_type=jnp.float32)
        other_term = None
        other_term = contract_rows(amplitudes, block_i)
        gamma_stack = gamma_stack.at[0].add(own_term)
        gamma_stack = gamma_stack.at[index].add(other_term)
    result = gamma_stack[:blocks]
    for hop in range(1, hops + 1):
        result = result + from_behind(
            gamma_stack[hop * blocks : (hop + 1) * blocks].astype(jnp.bfloat16), "occ", hop
        ).astype(jnp.float32)
    return result


def solution(mesh):
    return jax.shard_map(
        body,
        mesh=mesh,
        in_specs=(P("occ", None, "aux"), P("occ", None), P("occ", None), P("occ", None)),
        out_specs=P("occ", None, "aux"),
        check_vma=False,
    )
```

profile of v0, /device:TPU:32, one launch (start us, length us, event | category | flops | bytes accessed | tf_op | source)
XLA Modules:
  0.0 513.3 jit_solution(2496180509459191851)
XLA Ops:
  6.5 0.0 all-reduce.4.cloned.1.call-start
  6.5 6.7 %collective-permute-start = (bf16[1,1024,2048]{2,1,0:T(8,128)(2,1)}, bf16[1,1024,2048]{2,1,0:T(8,128)(2,1)}, u32[]{:S(2)}, u32[]{:S(2)}) collective-permute-start(bf16[1,1024,2048]{2,1,0:T(8,128)(2,1)} %param.12), channel_id=1, source_target_pairs={{2,0},{4,2},{6,4},{8,6},{10,8},{12,10},{14,12},{16,14},{18,16},{20... | collective-permute-start | bytes 12582920 | tf_op jit(solution)/shard_map/ppermute | solution.py:12
  13.2 2.7 collective-permute-start.1
  15.9 1.4 fusion.33
  18.7 2.5 constant_dynamic-update-slice_fusion.2
  21.2 172.1 %collective-permute-done = bf16[1,1024,2048]{2,1,0:T(8,128)(2,1)} collective-permute-done((bf16[1,1024,2048]{2,1,0:T(8,128)(2,1)}, bf16[1,1024,2048]{2,1,0:T(8,128)(2,1)}, u32[]{:S(2)}, u32[]{:S(2)}) %collective-permute-start) | collective-permute-done | bytes 4194336 | tf_op jit(solution)/shard_map/ppermute | solution.py:12
  193.2 2.5 constant_dynamic-update-slice_fusion.1
  195.7 0.0 copy-start.1
  195.7 0.0 collective-permute-done.1
  195.7 2.7 constant_dynamic-update-slice_fusion
  198.4 0.8 copy-done.1
  199.2 0.0 copy-start.2
  199.2 5.8 %convert_bitcast_fusion = bf16[1024,1024]{0,1:T(8,128)(2,1)} fusion(bf16[1,1024,2048]{2,1,0:T(8,128)(2,1)S(1)} %copy-done.1, bf16[3,1024,2048]{2,1,0:T(8,128)(2,1)S(1)} %constant_dynamic-update-slice_fusion, s32[]{:T(128)} %min.13), kind=kOutput, calls=%fused_computation.25 | convolution fusion | flops 4296015872 | bytes 10485764 | tf_op jit(solution)/shard_map/dot_general | solution.py:26
  205.0 0.0 copy-done.2
  205.0 5.7 %convert_bitcast_fusion.1 = bf16[1024,1024]{0,1:T(8,128)(2,1)} fusion(bf16[1,1024,2048]{2,1,0:T(8,128)(2,1)S(1)} %copy-done.1, bf16[3,1024,2048]{2,1,0:T(8,128)(2,1)S(1)} %constant_dynamic-update-slice_fusion, s32[]{:T(128)} %min.11), kind=kOutput, calls=%fused_computation.26 | convolution fusion | flops 4296015872 | bytes 10485764 | tf_op jit(solution)/shard_map/dot_general | solution.py:26
  210.7 0.0 all-reduce.4.cloned.1.call-update
  210.7 0.6 copy-done.4
  211.4 1.9 collective-permute-start.5
  213.3 8.6 %collective-permute-start.4 = (bf16[1,4]{1,0:T(2,128)(2,1)S(1)}, bf16[1,4]{1,0:T(2,128)(2,1)S(1)}, u32[]{:S(2)}, u32[]{:S(2)}) collective-permute-start(bf16[1,4]{1,0:T(2,128)(2,1)S(1)} %convert_element_type.58), channel_id=1, source_target_pairs={{2,0},{4,2},{6,4},{8,6},{10,8},{12,10},{14,12},{16,14},{18,16},{20... | collective-permute-start | bytes 32 | tf_op jit(solution)/shard_map/ppermute | solution.py:12
  221.9 0.0 copy-done.3
  221.9 2.9 collective-permute-start.3
  224.8 2.5 collective-permute-start.2
  228.7 0.1 subtract_bitcast_fusion.2
  228.8 0.0 copy-done.5
  228.8 0.8 and_reduce_fusion
  229.5 0.0 collective-permute-done.5
  229.6 0.0 collective-permute-done.4
  229.6 0.0 collective-permute-done.3
  229.6 0.7 collective-permute-done.2
  230.3 0.1 subtract_bitcast_fusion
  230.4 18.0 %all-reduce.4.cloned.1.call-done = (bf16[1024,1024]{0,1:T(8,128)(2,1)}, bf16[1024,1024]{0,1:T(8,128)(2,1)}) async-done(((bf16[1024,1024]{0,1:T(8,128)(2,1)}, bf16[1024,1024]{0,1:T(8,128)(2,1)}), (bf16[1024,1024]{0,1:T(8,128)(2,1)}, bf16[1024,1024]{0,1:T(8,128)(2,1)})) %all-reduce.4.cloned.1.call-update) | async-done | bytes 4194320 | tf_op jit(solution)/shard_map/psum | solution.py:60
  248.4 10.9 %convolution_bitcast_fusion = f32[1,1024,2048]{2,1,0:T(8,128)} fusion(bf16[3,1024,2048]{2,1,0:T(8,128)(2,1)} %copy-done.2, s32[]{:T(128)} %min.11, bf16[1024,1024]{0,1:T(8,128)(2,1)} %get-tuple-element.55, f32[1024]{0:T(1024)S(1)} %bitcast.67, f32[1024]{0:T(1024)S(1)} %bitcast.61, pred[]{:T(512)S(6)} %ge.6), kind=kOutput, calls=%fused_computation.8 | convolution fusion | flops 4300210176 | bytes 14688769 | tf_op jit(solution)/shard_map/dot_general | solution.py:66
  259.3 6.6 %scatter-add.14 = f32[3,1024,2048]{2,1,0:T(8,128)S(1)} pad(f32[1,1024,2048]{2,1,0:T(8,128)} %convolution_bitcast_fusion, f32[]{:T(128)} %constant.118.clone.1), padding=0_2x0_0x0_0 | pad | bytes 33554436 | tf_op jit(solution)/shard_map/scatter-add | solution.py:69
  266.0 0.0 copy-done.7
  266.0 0.0 copy-start.6
  266.0 8.2 %fusion = f32[3,1024,2048]{2,1,0:T(8,128)S(1)} fusion(f32[3,1024,2048]{2,1,0:T(8,128)S(1)} %scatter-add.14, s32[]{:T(128)} %min.11, bf16[1,1024,2048]{2,1,0:T(8,128)(2,1)} %param.12, pred[]{:T(512)} %get-tuple-element.54, bf16[1024,1024]{0,1:T(8,128)(2,1)S(1)} %copy-done.7, f32[1024]{0:T(1024)S(1)} %bitcast.68, f32[1024]{0:T(1024)S(1)} %bitcast.62, pred[]{:T(512)S(6)} %ge.6), kind=kOutput, calls=%fused_computation.2 | convolution fusion | flops 4304404480 | bytes 23076870 | tf_op jit(solution)/shard_map/dot_general | solution.py:20
  274.2 0.0 copy-done.6
  274.2 7.3 %fusion.3 = f32[3,1024,2048]{2,1,0:T(8,128)S(1)} fusion(f32[3,1024,2048]{2,1,0:T(8,128)S(1)} %fusion, bf16[3,1024,2048]{2,1,0:T(8,128)(2,1)} %copy-done.2, s32[]{:T(128)} %min.13, bf16[1024,1024]{0,1:T(8,128)(2,1)S(1)} %copy-done.6, f32[1024]{0:T(1024)S(1)} %bitcast.65, f32[1024]{0:T(1024)S(1)} %bitcast.63, pred[]{:T(512)S(6)} %ge.7), kind=kOutput, calls=%fused_computation.7 | convolution fusion | flops 4302307328 | bytes 23077376 | tf_op jit(solution)/shard_map/dot_general | solution.py:66
  281.5 8.1 %fusion.1 = f32[3,1024,2048]{2,1,0:T(8,128)S(1)} fusion(f32[3,1024,2048]{2,1,0:T(8,128)S(1)} %fusion.3, s32[]{:T(128)} %min.13, bf16[1,1024,2048]{2,1,0:T(8,128)(2,1)} %param.12, pred[]{:T(512)} %get-tuple-element.53, bf16[1024,1024]{0,1:T(8,128)(2,1)S(1)} %copy-done.6, f32[1024]{0:T(1024)S(1)} %bitcast.66, f32[1024]{0:T(1024)S(1)} %bitcast.64, pred[]{:T(512)S(6)} %ge.7), kind=kOutput, calls=%fused_computation.3 | convolution fusion | flops 4304404480 | bytes 23076870 | tf_op jit(solution)/shard_map/dot_general | solution.py:20
  289.6 0.0 copy-start
  289.6 7.6 %convert.4 = bf16[3,1024,2048]{2,1,0:T(8,128)(2,1)} convert(f32[3,1024,2048]{2,1,0:T(8,128)S(1)} %fusion.1) | non-fusion elementwise | flops 6291456 | bytes 37748736 | tf_op jit(solution)/shard_map/convert.1
  297.2 4.5 copy-done
  301.7 5.3 %fusion.32 = (bf16[1,1024,2048]{2,1,0:T(8,128)(2,1)}, bf16[1,1024,2048]{2,1,0:T(8,128)(2,1)S(1)}) fusion(bf16[3,1024,2048]{2,1,0:T(8,128)(2,1)} %convert.4), kind=kLoop, calls=%fused_computation.51 | loop fusion | bytes 16777216 | tf_op jit(solution)/shard_map/slice | solution.py:74
  307.0 3.3 collective-permute-start.6
  310.3 4.6 collective-permute-start.7
  315.0 91.7 %collective-permute-done.6 = bf16[1,1024,2048]{2,1,0:T(8,128)(2,1)S(1)} collective-permute-done((bf16[1,1024,2048]{2,1,0:T(8,128)(2,1)}, bf16[1,1024,2048]{2,1,0:T(8,128)(2,1)S(1)}, u32[]{:S(2)}, u32[]{:S(2)}) %collective-permute-start.6) | collective-permute-done | bytes 4194336 | tf_op jit(solution)/shard_map/ppermute | solution.py:12
  406.7 89.4 %collective-permute-done.7 = bf16[1,1024,2048]{2,1,0:T(8,128)(2,1)} collective-permute-done((bf16[1,1024,2048]{2,1,0:T(8,128)(2,1)S(1)}, bf16[1,1024,2048]{2,1,0:T(8,128)(2,1)}, u32[]{:S(2)}, u32[]{:S(2)}) %collective-permute-start.7) | collective-permute-done | bytes 4194336 | tf_op jit(solution)/shard_map/ppermute | solution.py:12
  496.1 10.4 %fusion.2 = f32[1,1024,2048]{2,1,0:T(8,128)} fusion(f32[3,1024,2048]{2,1,0:T(8,128)} %copy-done, bf16[1,1024,2048]{2,1,0:T(8,128)(2,1)} %collective-permute-done.7, bf16[1,1024,2048]{2,1,0:T(8,128)(2,1)S(1)} %collective-permute-done.6), kind=kLoop, calls=%fused_computation.5 | loop fusion | flops 8388608 | bytes 25165824 | tf_op jit(solution)/shard_map/add | solution.py:73
  (17 shorter events, 0.1 us)
Async XLA Ops:
  6.5 241.9 %all-reduce.4.cloned.1.call-start = ((), (), s32[]{:S(2)}) async-start(), calls=%async_computation | async-start | bytes 8388608 | tf_op jit(solution)/shard_map/psum | solution.py:60
  6.5 186.7 %collective-permute-start = (bf16[1,1024,2048]{2,1,0:T(8,128)(2,1)}, bf16[1,1024,2048]{2,1,0:T(8,128)(2,1)}, u32[]{:S(2)}, u32[]{:S(2)}) collective-permute-start(bf16[1,1024,2048]{2,1,0:T(8,128)(2,1)} %param.12), channel_id=1, source_target_pairs={{2,0},{4,2},{6,4},{8,6},{10,8},{12,10},{14,12},{16,14},{18,16},{20... | collective-permute-start | bytes 12582920 | tf_op jit(solution)/shard_map/ppermute | solution.py:12
  13.2 182.5 %collective-permute-start.1 = (bf16[1,1024,2048]{2,1,0:T(8,128)(2,1)}, bf16[1,1024,2048]{2,1,0:T(8,128)(2,1)}, u32[]{:S(2)}, u32[]{:S(2)}) collective-permute-start(bf16[1,1024,2048]{2,1,0:T(8,128)(2,1)} %param.12), channel_id=1, source_target_pairs={{4,0},{6,2},{8,4},{10,6},{12,8},{14,10},{16,12},{18,14},{20,16},{2... | collective-permute-start | bytes 12582920 | tf_op jit(solution)/shard_map/ppermute | solution.py:12
  195.7 3.5 copy-start.1
  199.2 5.8 %copy-start.2 = (bf16[3,1024,2048]{2,1,0:T(8,128)(2,1)}, bf16[3,1024,2048]{2,1,0:T(8,128)(2,1)S(1)}, u32[]{:S(2)}) copy-start(bf16[3,1024,2048]{2,1,0:T(8,128)(2,1)S(1)} %constant_dynamic-update-slice_fusion) | copy-start | bytes 37748740
  210.7 0.7 copy-start.4
  210.7 11.2 %copy-start.3 = (f32[1,256]{1,0:T(1,128)S(1)}, f32[1,256]{1,0:T(1,128)}, u32[]{:S(2)}) copy-start(f32[1,256]{1,0:T(1,128)} %param.14) | copy-start | bytes 3076
  210.7 18.1 %copy-start.5 = (s32[3]{0:T(128)S(1)}, s32[3]{0:T(128)}, u32[]{:S(2)}) copy-start(s32[3]{0:T(128)} %constant.120.clone.1) | copy-start | bytes 40
  211.4 18.2 %collective-permute-start.5 = (bf16[1,4]{1,0:T(2,128)(2,1)S(1)}, bf16[1,4]{1,0:T(2,128)(2,1)S(1)}, u32[]{:S(2)}, u32[]{:S(2)}) collective-permute-start(bf16[1,4]{1,0:T(2,128)(2,1)S(1)} %convert_element_type.58), channel_id=1, source_target_pairs={{4,0},{6,2},{8,4},{10,6},{12,8},{14,10},{16,12},{18,14},{20,16},{2... | collective-permute-start | bytes 32 | tf_op jit(solution)/shard_map/ppermute | solution.py:12
  213.3 16.3 %collective-permute-start.4 = (bf16[1,4]{1,0:T(2,128)(2,1)S(1)}, bf16[1,4]{1,0:T(2,128)(2,1)S(1)}, u32[]{:S(2)}, u32[]{:S(2)}) collective-permute-start(bf16[1,4]{1,0:T(2,128)(2,1)S(1)} %convert_element_type.58), channel_id=1, source_target_pairs={{2,0},{4,2},{6,4},{8,6},{10,8},{12,10},{14,12},{16,14},{18,16},{20... | collective-permute-start | bytes 32 | tf_op jit(solution)/shard_map/ppermute | solution.py:12
  221.9 7.7 %collective-permute-start.3 = (bf16[1,256]{1,0:T(2,128)(2,1)S(1)}, bf16[1,256]{1,0:T(2,128)(2,1)S(1)}, u32[]{:S(2)}, u32[]{:S(2)}) collective-permute-start(bf16[1,256]{1,0:T(2,128)(2,1)S(1)} %convert_element_type.55), channel_id=1, source_target_pairs={{4,0},{6,2},{8,4},{10,6},{12,8},{14,10},{16,12},{18,14},{20,16},{2... | collective-permute-start | bytes 1544 | tf_op jit(solution)/shard_map/ppermute | solution.py:12
  224.8 5.5 %collective-permute-start.2 = (bf16[1,256]{1,0:T(2,128)(2,1)S(1)}, bf16[1,256]{1,0:T(2,128)(2,1)S(1)}, u32[]{:S(2)}, u32[]{:S(2)}) collective-permute-start(bf16[1,256]{1,0:T(2,128)(2,1)S(1)} %convert_element_type.55), channel_id=1, source_target_pairs={{2,0},{4,2},{6,4},{8,6},{10,8},{12,10},{14,12},{16,14},{18,16},{20... | collective-permute-start | bytes 1544 | tf_op jit(solution)/shard_map/ppermute | solution.py:12
  259.3 6.6 %copy-start.7 = (bf16[1024,1024]{0,1:T(8,128)(2,1)S(1)}, bf16[1024,1024]{0,1:T(8,128)(2,1)}, u32[]{:S(2)}) copy-start(bf16[1024,1024]{0,1:T(8,128)(2,1)} %get-tuple-element.55) | copy-start | bytes 6291460
  266.0 8.2 %copy-start.6 = (bf16[1024,1024]{0,1:T(8,128)(2,1)S(1)}, bf16[1024,1024]{0,1:T(8,128)(2,1)}, u32[]{:S(2)}) copy-start(bf16[1024,1024]{0,1:T(8,128)(2,1)} %get-tuple-element.56) | copy-start | bytes 6291460
  289.6 12.1 %copy-start = (f32[3,1024,2048]{2,1,0:T(8,128)}, f32[3,1024,2048]{2,1,0:T(8,128)S(1)}, u32[]{:S(2)}) copy-start(f32[3,1024,2048]{2,1,0:T(8,128)S(1)} %fusion.1) | copy-start | bytes 75497472
  307.0 99.7 %collective-permute-start.6 = (bf16[1,1024,2048]{2,1,0:T(8,128)(2,1)}, bf16[1,1024,2048]{2,1,0:T(8,128)(2,1)S(1)}, u32[]{:S(2)}, u32[]{:S(2)}) collective-permute-start(bf16[1,1024,2048]{2,1,0:T(8,128)(2,1)} %get-tuple-element.57), channel_id=1, source_target_pairs={{0,2},{2,4},{4,6},{6,8},{8,10},{10,12},{12,14},{14,16},{16,18},{18... | collective-permute-start | bytes 12582920 | tf_op jit(solution)/shard_map/ppermute | solution.py:12
  310.3 185.7 %collective-permute-start.7 = (bf16[1,1024,2048]{2,1,0:T(8,128)(2,1)S(1)}, bf16[1,1024,2048]{2,1,0:T(8,128)(2,1)}, u32[]{:S(2)}, u32[]{:S(2)}) collective-permute-start(bf16[1,1024,2048]{2,1,0:T(8,128)(2,1)S(1)} %get-tuple-element.58), channel_id=1, source_target_pairs={{0,4},{2,6},{4,8},{6,10},{8,12},{10,14},{12,16},{14,18},{16,20},{1... | collective-permute-start | bytes 12582920 | tf_op jit(solution)/shard_map/ppermute | solution.py:12
Sparse Core Ops, SparseCore 0:
  210.8 37.5 all-reduce.3
where the time goes:
time: 514 us; the launch traced here: 513 us
  waiting for transfers between devices  372 us (72%)
  matrix products  46 us (9%)
  starting transfers between devices  33.2 us (6%)
  local copies, waits for them, and re-layouts  26.9 us (5%)
  other arithmetic  19 us (4%)
  between operations  16.3 us (3%)
    ppermute x8, waiting for transfers between devices, from_behind(): return lax.ppermute(array, axis, pairs)  354 us
    ppermute x8, starting transfers between devices, from_behind(): return lax.ppermute(array, axis, pairs)  33.2 us
    dot_general x2, matrix products, body(): own_term = jnp.dot(amplitudes, block_j, preferred_element_type=jnp.float32)  18.2 us
    psum x1, waiting for transfers between devices, body(): lax.psum(contract_cols(block_i, block_j).astype(jnp.bfloat16), 'aux')  18 us
    dot_general x2, matrix products, contract_rows(): lax.dot_general(left, right, (((0,), (0,)), ((), ())), preferred_element_...  16.3 us
    dot_general x2, matrix products, contract_cols(): lax.dot_general(left, right, (((1,), (1,)), ((), ())), preferred_element_...  11.5 us
    unnamed x21, local copies, waits for them, and re-layouts  10.9 us
    add x1, other arithmetic, body(): result + from_behind(gamma_stack[hop * blocks:(hop + 1) * blocks].astype(...  10.4 us
  transfers between devices with their start and end apart: 9, of which 5 were waited for; matrix products, arithmetic and copies ran while one was open for 1% of the time, Pallas kernels for 0%

commit v1 on v0

v1 whole, which is shorter than its diff:
```python
import functools

import jax
import jax.numpy as jnp
from jax import lax
from jax.experimental import pallas as pl
from jax.experimental.pallas import tpu as pltpu
from jax.sharding import PartitionSpec as P

MESH = pl.DeviceIdType.MESH
RING = 4
STEPS = 16
LEFT, RIGHT, FAR, CROSS, WRAP, RELAY, CHUNKS = 0, 8, 16, 24, 32, 36, 40

NT = (((1,), (1,)), ((), ()))


def kernel(
    n, ints_ref, occ_ref, vir_ref, par_ref, out_ref,
    own, nb, gamma, pbuf, xsend, xrecv, abuf, levcol, meta_own, meta_nb,
    send_sem, recv_sem, xs_sem, xr_sem, ms_sem, mr_sem, own_sem, out_sem,
):
    rows, aux = ints_ref.shape
    chunk = rows // 8
    step_rows = rows // 4
    virt = vir_ref.shape[1]
    me = lax.axis_index("occ")
    core = lax.axis_index("aux")
    x = me % RING
    right = me - x + (x + 1) % RING
    left = me - x + (x + RING - 1) % RING
    ymain = (me + n + RING - 2 * RING * (x // 2)) % n
    yback = (me + n - RING + 2 * RING * (x // 2)) % n
    near = ((me + 1) % n, (me + n - 1) % n, (me + 2) % n, (me + n - 2) % n)
    edge = (x == 0) | (x == RING - 1)

    def own_chunk(i):
        return ints_ref.at[pl.ds(pl.multiple_of(i * chunk, chunk), chunk)]

    def nb_chunk(i):
        return nb.at[pl.ds(pl.multiple_of(i * chunk, chunk), chunk)]

    def copy(src, to, ssem, device):
        return pltpu.make_async_remote_copy(
            src_ref=src, dst_ref=nb_chunk(to), send_sem=send_sem.at[ssem], recv_sem=recv_sem.at[to],
            device_id=(device, core), device_id_type=MESH,
        )

    def arrive(i):
        copy(nb_chunk(i), i, 0, right).wait_recv()

    def meta_copy(k, device):
        return pltpu.make_async_remote_copy(
            src_ref=meta_own, dst_ref=meta_nb.at[k], send_sem=ms_sem.at[k], recv_sem=mr_sem.at[k],
            device_id=(device, core), device_id_type=MESH,
        )

    def exchange(s):
        return pltpu.make_async_remote_copy(
            src_ref=xsend.at[s % 2], dst_ref=xrecv.at[s], send_sem=xs_sem.at[s], recv_sem=xr_sem.at[s],
            device_id=(me, 1 - core), device_id_type=MESH,
        )

    load = pltpu.make_async_copy(ints_ref, own, own_sem)
    load.start()

    barrier = pltpu.get_barrier_semaphore()
    for device in (right, left, ymain, yback, *near):
        pl.semaphore_signal(barrier, inc=1, device_id=(device, core), device_id_type=MESH)
    pl.semaphore_signal(barrier, inc=1, device_id=(me, 1 - core), device_id_type=MESH)
    pl.semaphore_wait(barrier, 9)

    @pl.loop(0, 4)
    def _(i):
        copy(own_chunk(i), LEFT + i, i, right).start()
        copy(own_chunk(4 + i), RIGHT + 4 + i, 12 + i, left).start()

        @pl.when(edge)
        def _():
            copy(own_chunk(4 * (x // 2) + i), RELAY + i, 36 + i, yback).start()

    for i in range(rows // virt):
        meta_own[0:1, i * virt : (i + 1) * virt] = vir_ref[...] - occ_ref[0, i]
    for reach in (1, 2):
        listed = (par_ref[0, 0] == me + reach) | (par_ref[0, 1] == me + reach)
        meta_own[reach : reach + 1, :] = jnp.full((1, rows), jnp.where(listed, 1.0, 0.0), jnp.float32)
    meta_own[3:8, :] = jnp.zeros((5, rows), jnp.float32)
    for k, device in enumerate(near):
        meta_copy(k, device).start()
    levcol[...] = jnp.broadcast_to(meta_own[0:1, :], (levcol.shape[1], rows)).T

    @pl.loop(0, 4)
    def _(i):
        here = pl.ds(pl.multiple_of(i * step_rows, step_rows), step_rows)
        gamma[here] = jnp.zeros((step_rows, aux), jnp.float32)

    for k in range(4):
        meta_copy(k, right).wait_recv()
    meta_nb[0, 3:4, :] = meta_nb[0, 1:2, :]
    meta_nb[1, 3:4, :] = meta_own[1:2, :]
    meta_nb[2, 3:4, :] = meta_nb[2, 2:3, :]
    meta_nb[3, 3:4, :] = meta_own[2:3, :]
    load.wait()

    def pass_along_ring(i):
        arrive(LEFT + i)
        copy(nb_chunk(LEFT + i), FAR + i, 4 + i, right).start()
        arrive(RIGHT + 4 + i)
        copy(nb_chunk(RIGHT + 4 + i), FAR + 4 + i, 16 + i, left).start()

        @pl.when(edge)
        def _():
            copy(nb_chunk(4 * x + i), WRAP + i, 32 + i, ymain).start()

    def rest_of_own(i):
        @pl.when(x < RING - 1)
        def _():
            copy(own_chunk(4 + i), LEFT + 4 + i, 8 + i, right).start()

        @pl.when(x > 0)
        def _():
            copy(own_chunk(i), RIGHT + i, 20 + i, left).start()

        @pl.when(edge)
        def _():
            arrive(RELAY + i)

        @pl.when(x == RING - 1)
        def _():
            copy(nb_chunk(RELAY + i), LEFT + 4 + i, 8 + i, right).start()

        @pl.when(x == 0)
        def _():
            copy(nb_chunk(RELAY + i), RIGHT + i, 20 + i, left).start()

    def pass_across(i):
        arrive(FAR + i)
        copy(nb_chunk(FAR + i), CROSS + i, 24 + i, ymain).start()
        arrive(FAR + 4 + i)
        copy(nb_chunk(FAR + 4 + i), CROSS + 4 + i, 28 + i, ymain).start()

    first = 1 - (x + 3) // 4
    last = (x + 1) // 4

    def place(s):
        early = 1 - s // 8
        quad0 = 1 - (s // 4 + 3) // 4
        quad1 = early - quad0
        h = s % 2
        late = s // 8
        kind = s % 4
        pair = kind // 2
        part = 2 * (early * ((s // 2) % 2) + late * ((s // 4) % 2))
        swap = (1 - h) * first + h * last
        at0 = (1 - swap) * (h * (RIGHT + 4)) + swap * WRAP
        in0 = 4 * h
        at1 = FAR + 4 * h
        at2 = (1 - pair) * (CROSS + 4 * h) + pair * ((1 - h) * (LEFT + 4) + h * RIGHT)
        in2 = (1 - pair) * (4 * h) + pair * (4 * (1 - h))
        at = quad0 * at0 + quad1 * at1 + late * at2 + part
        inside = quad0 * in0 + quad1 * (4 * h) + late * in2 + part
        slot = quad0 * h + quad1 * (3 - x // 2) + late * ((1 - pair) * (2 + x // 2) + pair * h)
        waits = quad0 * swap + late
        return at, inside, slot, waits

    def block_rows(at):
        return pl.ds(pl.multiple_of(at * chunk, chunk), step_rows)

    m_rows = rows // 2
    n_cols = aux // 4

    def products(s):
        at, inside, slot, waits = place(s)

        @pl.when(waits == 1)
        def _():
            arrive(at)
            arrive(at + 1)

        @pl.when(s >= 2)
        def _():
            exchange(s - 2).wait_send()

        @pl.loop(0, rows // m_rows)
        def _(m):
            here = pl.ds(pl.multiple_of(m * m_rows, m_rows), m_rows)
            part = lax.dot_general(own[here], nb[block_rows(at)], NT, preferred_element_type=jnp.float32)
            pbuf[s % 2, here] = part
            xsend[s % 2, here] = part.astype(jnp.bfloat16)

        exchange(s).start()

    def finish(s):
        at, inside, slot, waits = place(s)
        exchange(s).wait_recv()
        cols = pl.ds(pl.multiple_of(inside * chunk, chunk), step_rows)
        level = meta_nb[slot, 0:1, cols]
        live = meta_nb[slot, 3:4, cols]
        wide = step_rows // levcol.shape[1]

        @pl.loop(0, 4)
        def _(m):
            here = pl.ds(pl.multiple_of(m * step_rows, step_rows), step_rows)
            total = pbuf[s % 2, here] + xrecv[s, here].astype(jnp.float32)
            mine = levcol[here]
            mine = jnp.concatenate([mine] * wide, axis=1)
            abuf[here] = jnp.where(live > 0.5, total / (mine + level), 0.0).astype(jnp.bfloat16)

        @pl.loop(0, aux // n_cols)
        def _(c):
            there = pl.ds(pl.multiple_of(c * n_cols, n_cols), n_cols)
            gamma[:, there] += jnp.dot(abuf[...], nb[block_rows(at), there], preferred_element_type=jnp.float32)

    @pl.loop(0, STEPS + 1)
    def _(s):
        @pl.when(s == 0)
        def _():
            pl.loop(0, 3)(pass_along_ring)

        @pl.when(s == 2)
        def _():
            pl.loop(3, 4)(pass_along_ring)
            pl.loop(0, 4)(rest_of_own)

        @pl.when(s == 4)
        def _():
            pl.loop(0, 2)(pass_across)

        @pl.when(s == 6)
        def _():
            pl.loop(2, 4)(pass_across)

        @pl.when(s < STEPS)
        def _():
            products(s)

        @pl.when(s >= 1)
        def _():
            finish(s - 1)

    store = pltpu.make_async_copy(gamma, out_ref, out_sem)
    store.start()

    @pl.loop(0, 32)
    def _(k):
        copy(nb_chunk(0), 0, k, right).wait_send()

    @pl.when(edge)
    def _():
        @pl.loop(32, 40)
        def _(k):
            copy(nb_chunk(0), 0, k, right).wait_send()

    for k in range(4):
        meta_copy(k, right).wait_send()
    exchange(STEPS - 2).wait_send()
    exchange(STEPS - 1).wait_send()
    store.wait()


def body(n, ints, occ_energy, vir_energy, partners):
    _, rows, aux = ints.shape
    lanes = min(128, rows // 4)
    step_rows = rows // 4
    result = pl.pallas_call(
        functools.partial(kernel, n),
        out_shape=jax.ShapeDtypeStruct((rows, aux), jnp.float32),
        in_specs=[
            pl.BlockSpec(memory_space=pl.ANY),
            pl.BlockSpec(memory_space=pltpu.SMEM),
            pl.BlockSpec(memory_space=pltpu.VMEM),
            pl.BlockSpec(memory_space=pltpu.SMEM),
        ],
        out_specs=pl.BlockSpec(memory_space=pl.ANY),
        scratch_shapes=[
            pltpu.VMEM((rows, aux), jnp.bfloat16),
            pltpu.VMEM((CHUNKS * rows // 8, aux), jnp.bfloat16),
            pltpu.VMEM((rows, aux), jnp.float32),
            pltpu.VMEM((2, rows, step_rows), jnp.float32),
            pltpu.VMEM((2, rows, step_rows), jnp.bfloat16),
            pltpu.VMEM((STEPS, rows, step_rows), jnp.bfloat16),
            pltpu.VMEM((rows, step_rows), jnp.bfloat16),
            pltpu.VMEM((rows, lanes), jnp.float32),
            pltpu.VMEM((8, rows), jnp.float32),
            pltpu.VMEM((4, 8, rows), jnp.float32),
            pltpu.SemaphoreType.DMA((40,)),
            pltpu.SemaphoreType.DMA((CHUNKS,)),
            pltpu.SemaphoreType.DMA((STEPS,)),
            pltpu.SemaphoreType.DMA((STEPS,)),
            pltpu.SemaphoreType.DMA((4,)),
            pltpu.SemaphoreType.DMA((4,)),
            pltpu.SemaphoreType.DMA,
            pltpu.SemaphoreType.DMA,
        ],
        compiler_params=pltpu.CompilerParams(
            collective_id=0, has_side_effects=True, vmem_limit_bytes=56 * 2**20
        ),
        cost_estimate=pl.CostEstimate(
            flops=16 * rows * rows * aux, bytes_accessed=6 * rows * aux, transcendentals=0
        ),
    )(ints[0], occ_energy, vir_energy, partners)
    return result[None]


def solution(mesh):
    return jax.shard_map(
        functools.partial(body, mesh.shape["occ"]),
        mesh=mesh,
        in_specs=(P("occ", None, "aux"), P("occ", None), P("occ", None), P("occ", None)),
        out_specs=P("occ", None, "aux"),
        check_vma=False,
    )
```

time: 514 us -> 227 us (0.44)
  waiting for transfers between devices: 372 us -> 0 us
  Pallas kernels: 0 us -> 218 us
  matrix products: 46 us -> 0 us
  starting transfers between devices: 33.2 us -> 0 us
  local copies, waits for them, and re-layouts: 26.9 us -> 7.89 us
  other arithmetic: 19 us -> 0 us
  between operations: 16.3 us -> 0.01 us
    ppermute x8 -> x0, waiting for transfers between devices: 354 us -> none  [from_behind(): return lax.ppermute(array, axis, pairs)]
    pallas_call x0 -> x1, Pallas kernels: none -> 218 us  [body(): pl.pallas_call(functools.partial(kernel, n), out_shape=jax.ShapeDtypeStru...]
    dot_general x6 -> x0, matrix products: 46 us -> none  [the longest x2 18.2 us: body(): own_term = jnp.dot(amplitudes, block_j, preferred_element_type=jnp.float32)]
    ppermute x8 -> x0, starting transfers between devices: 33.2 us -> none  [from_behind(): return lax.ppermute(array, axis, pairs)]
    psum x1 -> x0, waiting for transfers between devices: 18 us -> none  [body(): lax.psum(contract_cols(block_i, block_j).astype(jnp.bfloat16), 'aux')]
    add x1 -> x0, other arithmetic: 10.4 us -> none  [body(): result + from_behind(gamma_stack[hop * blocks:(hop + 1) * blocks].astype(...]
    another operation x2 -> x0, other arithmetic: 8.39 us -> none
    slice x2 -> x0, local copies, waits for them, and re-layouts: 6.72 us -> none  [the longest x1 5.32 us: body(): gamma_stack[hop * blocks:(hop + 1) * blocks].astype(jnp.bfloat16)]
  transfers between devices with their start and end apart: 9 -> 0, of which waited for: 5 -> 0; matrix products, arithmetic and copies ran while one was open for 1% -> 0% of each run, Pallas kernels for 0% -> 0%
where the time goes in v1:
time: 227 us; the launch traced here: 226 us
  Pallas kernels  218 us (96%)
  local copies, waits for them, and re-layouts  7.89 us (3%)
    pallas_call x1, Pallas kernels, body(): pl.pallas_call(functools.partial(kernel, n), out_shape=jax.ShapeDtypeStru...  218 us
    unnamed x1, local copies, waits for them, and re-layouts  7.89 us

profile of v1, /device:TPU:32, one launch (start us, length us, event | category | flops | bytes accessed | tf_op | source)
XLA Modules:
  0.0 225.6 jit_solution(3388336313343312409)
XLA Ops:
  0.0 217.8 %shard_map.46 = f32[1024,2048]{1,0:T(8,128)} custom-call(bf16[1024,2048]{1,0:T(8,128)(2,1)} %bitcast.3, f32[1,4]{1,0:T(1,128)} %occ_ref.1, f32[1,256]{1,0:T(1,128)} %vir_ref.1, s32[1,2]{1,0:T(1,128)} %par_ref.1), custom_call_target="tpu_custom_call" | custom-call | flops 34359738368 | bytes 12582912 | tf_op jit(solution)/shard_map/pallas_call | solution.py:265
  217.8 7.9 %copy.6 = f32[1,1024,2048]{2,1,0:T(8,128)} copy(f32[1,1024,2048]{2,1,0:T(8,128)} %bitcast.2) | data formatting | bytes 16777216

commit v2 on v1

v2 whole, which is shorter than its diff:
```python
import functools

import jax
import jax.numpy as jnp
from jax import lax
from jax.experimental import pallas as pl
from jax.experimental.pallas import tpu as pltpu
from jax.sharding import PartitionSpec as P

MESH = pl.DeviceIdType.MESH
RING = 4
PARTS = 16
HALF = PARTS // 2
TICKS = 3 * HALF
AHEAD = 2
STEPS = 18
LEFT, RIGHT, FAR, CROSS, WRAP, RELAY, CHUNKS = 0, 16, 32, 48, 64, 72, 80
TO_RIGHT, TO_LEFT, TO_CROSS, TO_WRAP, TO_RELAY, SENDS = 0, 24, 48, 64, 72, 80

NT = (((1,), (1,)), ((), ()))


def kernel(
    n, ints_ref, occ_ref, vir_ref, par_ref, gamma,
    own, nb, pbuf, xsend, xrecv, abuf, levcol, meta_own, meta_nb,
    send_sem, recv_sem, xs_sem, xr_sem, ms_sem, mr_sem, own_sem,
):
    rows, aux = ints_ref.shape
    chunk = rows // PARTS
    step_rows = rows // 4
    virt = vir_ref.shape[1]
    me = lax.axis_index("occ")
    core = lax.axis_index("aux")
    x = me % RING
    right = me - x + (x + 1) % RING
    left = me - x + (x + RING - 1) % RING
    ymain = (me + n + RING - 2 * RING * (x // 2)) % n
    yback = (me + n - RING + 2 * RING * (x // 2)) % n
    near = ((me + 1) % n, (me + n - 1) % n, (me + 2) % n, (me + n - 2) % n)
    edge = (x == 0) | (x == RING - 1)

    def own_chunk(i):
        return ints_ref.at[pl.ds(pl.multiple_of(i * chunk, chunk), chunk)]

    def nb_chunk(i):
        return nb.at[pl.ds(pl.multiple_of(i * chunk, chunk), chunk)]

    def copy(src, to, ssem, device):
        return pltpu.make_async_remote_copy(
            src_ref=src, dst_ref=nb_chunk(to), send_sem=send_sem.at[ssem], recv_sem=recv_sem.at[to],
            device_id=(device, core), device_id_type=MESH,
        )

    def arrive(i):
        copy(nb_chunk(i), i, 0, right).wait_recv()

    def meta_copy(k, device):
        return pltpu.make_async_remote_copy(
            src_ref=meta_own, dst_ref=meta_nb.at[k], send_sem=ms_sem.at[k], recv_sem=mr_sem.at[k],
            device_id=(device, core), device_id_type=MESH,
        )

    def exchange(t):
        step = 3 * (t // 4 - 1) + t % 4
        return pltpu.make_async_remote_copy(
            src_ref=xsend.at[t % 4], dst_ref=xrecv.at[step], send_sem=xs_sem.at[step], recv_sem=xr_sem.at[step],
            device_id=(me, 1 - core), device_id_type=MESH,
        )

    load = pltpu.make_async_copy(ints_ref, own, own_sem)
    load.start()

    barrier = pltpu.get_barrier_semaphore()
    for device in (right, left, ymain, yback, *near):
        pl.semaphore_signal(barrier, inc=1, device_id=(device, core), device_id_type=MESH)
    pl.semaphore_signal(barrier, inc=1, device_id=(me, 1 - core), device_id_type=MESH)
    pl.semaphore_wait(barrier, 9)

    def send_on_ring(k):
        @pl.when(k < HALF)
        def _():
            copy(own_chunk(k), LEFT + k, TO_RIGHT + k, right).start()
            copy(own_chunk(HALF + k), RIGHT + HALF + k, TO_LEFT + k, left).start()

        @pl.when((k >= HALF) & (k < 2 * HALF))
        def _():
            i = k - HALF
            copy(nb_chunk(LEFT + i), FAR + i, TO_RIGHT + k, right).start()
            copy(nb_chunk(RIGHT + HALF + i), FAR + HALF + i, TO_LEFT + k, left).start()

        @pl.when((k >= 2 * HALF) & (k < TICKS))
        def _():
            i = k - 2 * HALF

            @pl.when(x < RING - 1)
            def _():
                copy(own_chunk(HALF + i), LEFT + HALF + i, TO_RIGHT + k, right).start()

            @pl.when(x > 0)
            def _():
                copy(own_chunk(i), RIGHT + i, TO_LEFT + k, left).start()

            @pl.when(edge)
            def _():
                arrive(RELAY + i)

            @pl.when(x == RING - 1)
            def _():
                copy(nb_chunk(RELAY + i), LEFT + HALF + i, TO_RIGHT + k, right).start()

            @pl.when(x == 0)
            def _():
                copy(nb_chunk(RELAY + i), RIGHT + i, TO_LEFT + k, left).start()

    pl.loop(0, AHEAD)(send_on_ring)

    @pl.when(edge)
    def _():
        @pl.loop(0, HALF)
        def _(i):
            copy(own_chunk(HALF * (x // 2) + i), RELAY + i, TO_RELAY + i, yback).start()

    for i in range(rows // virt):
        meta_own[0:1, i * virt : (i + 1) * virt] = vir_ref[...] - occ_ref[0, i]
    for reach in (1, 2):
        listed = (par_ref[0, 0] == me + reach) | (par_ref[0, 1] == me + reach)
        meta_own[reach : reach + 1, :] = jnp.full((1, rows), jnp.where(listed, 1.0, 0.0), jnp.float32)
    meta_own[3:8, :] = jnp.zeros((5, rows), jnp.float32)
    for k, device in enumerate(near):
        meta_copy(k, device).start()
    levcol[...] = jnp.broadcast_to(meta_own[0:1, :], (levcol.shape[1], rows)).T

    @pl.loop(0, 4)
    def _(i):
        here = pl.ds(pl.multiple_of(i * step_rows, step_rows), step_rows)
        gamma[here] = jnp.zeros((step_rows, aux), jnp.float32)

    for k in range(4):
        meta_copy(k, right).wait_recv()
    meta_nb[0, 3:4, :] = meta_nb[0, 1:2, :]
    meta_nb[1, 3:4, :] = meta_own[1:2, :]
    meta_nb[2, 3:4, :] = meta_nb[2, 2:3, :]
    meta_nb[3, 3:4, :] = meta_own[2:3, :]
    load.wait()

    def send_across(j):
        i = HALF * ((j // 4) % 2) + 4 * (j // 8) + j % 4
        copy(nb_chunk(FAR + i), CROSS + i, TO_CROSS + j, ymain).start()

    def links(t):
        @pl.when(t < 2 * HALF)
        def _():
            arrive(LEFT + t + (t // HALF) * (FAR - LEFT - HALF))
            arrive(RIGHT + HALF + t + (t // HALF) * (FAR - RIGHT - HALF))

        @pl.when(edge & (t < HALF))
        def _():
            copy(nb_chunk((RIGHT + HALF) // 3 * x + t), WRAP + t, TO_WRAP + t, ymain).start()

        @pl.when((t >= HALF) & (t < HALF + 4))
        def _():
            send_across(t - HALF)

        @pl.when((t >= HALF + 3) & (t < 3 * HALF - 1))
        def _():
            send_across(t - HALF + 1)

        copy(nb_chunk(0), 0, TO_RIGHT + t, right).wait_send()
        copy(nb_chunk(0), 0, TO_LEFT + t, left).wait_send()
        send_on_ring(t + AHEAD)

    first = 1 - (x + 3) // 4
    last = (x + 1) // 4

    def has_step(t):
        return (t >= 5) & (t < 27) & (t % 4 < 3) & ((t >= 12) | (t % 4 > 0))

    def place(t):
        q, r = t // 4, t % 4
        q12 = (8 - q) // 6
        q56 = (q + 1) // 6
        q34 = 1 - q12 - q56
        r2 = r // 2
        r1 = r % 2
        r0 = 1 - r1 - r2
        swap = r1 * first + r2 * last
        across = (1 - q12) * r2
        g = q - 3
        at = (
            q12 * (r2 * (1 - swap) * (RIGHT + HALF) + swap * WRAP + 4 * (q - 1))
            + across * (CROSS + HALF * (g % 2) + 4 * (g // 2))
            + q34 * (1 - r2) * (FAR + HALF * r1 + 4 * (q - 3))
            + q56 * (1 - r2) * (r0 * (LEFT + HALF) + r1 * RIGHT + 4 * (q - 5))
        )
        inside = (
            q12 * (r2 * HALF + 4 * (q - 1))
            + across * (HALF * (g % 2) + 4 * (g // 2))
            + q34 * (1 - r2) * (HALF * r1 + 4 * (q - 3))
            + q56 * (1 - r2) * (r0 * HALF + 4 * (q - 5))
        )
        slot = q12 * r2 + across * (2 + x // 2) + q34 * (1 - r2) * (3 - x // 2) + q56 * (1 - r2) * r1
        waits = q12 * swap + across + q56 * (1 - r2)
        return at, inside, slot, waits

    def block_rows(at):
        return pl.ds(pl.multiple_of(at * chunk, chunk), step_rows)

    m_rows = rows // 2
    n_cols = aux // 4

    def products(t):
        at, inside, slot, waits = place(t)

        @pl.when(waits == 1)
        def _():
            pl.loop(0, 4)(lambda i: arrive(at + i))

        @pl.when(has_step(t - 4))
        def _():
            exchange(t - 4).wait_send()

        @pl.loop(0, rows // m_rows)
        def _(m):
            here = pl.ds(pl.multiple_of(m * m_rows, m_rows), m_rows)
            part = lax.dot_general(own[here], nb[block_rows(at)], NT, preferred_element_type=jnp.float32)
            pbuf[t % 4, here] = part
            xsend[t % 4, here] = part.astype(jnp.bfloat16)

        exchange(t).start()

    def finish(t):
        at, inside, slot, waits = place(t)
        exchange(t).wait_recv()
        cols = pl.ds(pl.multiple_of(inside * chunk, step_rows), step_rows)
        level = meta_nb[slot, 0:1, cols]
        live = meta_nb[slot, 3:4, cols]
        wide = step_rows // levcol.shape[1]
        step = 3 * (t // 4 - 1) + t % 4

        @pl.loop(0, 4)
        def _(m):
            here = pl.ds(pl.multiple_of(m * step_rows, step_rows), step_rows)
            total = pbuf[t % 4, here] + xrecv[step, here].astype(jnp.float32)
            mine = levcol[here]
            mine = jnp.concatenate([mine] * wide, axis=1)
            abuf[here] = jnp.where(live > 0.5, total / (mine + level), 0.0).astype(jnp.bfloat16)

        @pl.loop(0, aux // n_cols)
        def _(c):
            there = pl.ds(pl.multiple_of(c * n_cols, n_cols), n_cols)
            gamma[:, there] += jnp.dot(abuf[...], nb[block_rows(at), there], preferred_element_type=jnp.float32)

    @pl.loop(0, 28)
    def _(t):
        @pl.when(t < TICKS)
        def _():
            links(t)

        @pl.when(has_step(t))
        def _():
            products(t)

        @pl.when(has_step(t - 1))
        def _():
            finish(t - 1)

    @pl.loop(TO_CROSS, TO_WRAP)
    def _(k):
        copy(nb_chunk(0), 0, k, right).wait_send()

    @pl.when(edge)
    def _():
        @pl.loop(TO_WRAP, SENDS)
        def _(k):
            copy(nb_chunk(0), 0, k, right).wait_send()

    for k in range(4):
        meta_copy(k, right).wait_send()
    for t in (24, 25, 26):
        exchange(t).wait_send()


def body(n, ints, occ_energy, vir_energy, partners):
    _, rows, aux = ints.shape
    lanes = min(128, rows // 4)
    step_rows = rows // 4
    result = pl.pallas_call(
        functools.partial(kernel, n),
        out_shape=pltpu.VMEM((rows, aux), jnp.float32),
        in_specs=[
            pl.BlockSpec(memory_space=pl.ANY),
            pl.BlockSpec(memory_space=pltpu.SMEM),
            pl.BlockSpec(memory_space=pltpu.VMEM),
            pl.BlockSpec(memory_space=pltpu.SMEM),
        ],
        out_specs=pl.BlockSpec(memory_space=pltpu.VMEM),
        scratch_shapes=[
            pltpu.VMEM((rows, aux), jnp.bfloat16),
            pltpu.VMEM((CHUNKS * rows // PARTS, aux), jnp.bfloat16),
            pltpu.VMEM((3, rows, step_rows), jnp.float32),
            pltpu.VMEM((3, rows, step_rows), jnp.bfloat16),
            pltpu.VMEM((STEPS, rows, step_rows), jnp.bfloat16),
            pltpu.VMEM((rows, step_rows), jnp.bfloat16),
            pltpu.VMEM((rows, lanes), jnp.float32),
            pltpu.VMEM((8, rows), jnp.float32),
            pltpu.VMEM((4, 8, rows), jnp.float32),
            pltpu.SemaphoreType.DMA((SENDS,)),
            pltpu.SemaphoreType.DMA((CHUNKS,)),
            pltpu.SemaphoreType.DMA((STEPS,)),
            pltpu.SemaphoreType.DMA((STEPS,)),
            pltpu.SemaphoreType.DMA((4,)),
            pltpu.SemaphoreType.DMA((4,)),
            pltpu.SemaphoreType.DMA,
        ],
        compiler_params=pltpu.CompilerParams(
            collective_id=0, has_side_effects=True, vmem_limit_bytes=44 * 2**20
        ),
        cost_estimate=pl.CostEstimate(
            flops=16 * rows * rows * aux, bytes_accessed=6 * rows * aux, transcendentals=0
        ),
    )(ints[0], occ_energy, vir_energy, partners)
    return result[None]


def solution(mesh):
    return jax.shard_map(
        functools.partial(body, mesh.shape["occ"]),
        mesh=mesh,
        in_specs=(P("occ", None, "aux"), P("occ", None), P("occ", None), P("occ", None)),
        out_specs=P("occ", None, "aux"),
        check_vma=False,
    )
```

time: 227 us -> 175 us (0.77)
  the two profiles are of different devices: /device:TPU:32 before, /device:TPU:1 now
where the time goes in v2:
time: 175 us
  Pallas kernels  170 us (97%)
  local copies, waits for them, and re-layouts  5.39 us (3%)
    pallas_call x1, Pallas kernels, body(): pl.pallas_call(functools.partial(kernel, n), out_shape=pltpu.VMEM((rows,...  170 us
    unnamed x7, local copies, waits for them, and re-layouts  5.39 us

profile of v2, /device:TPU:1, one launch (start us, length us, event | category | flops | bytes accessed | tf_op | source)
XLA Modules:
  0.0 175.3 jit_solution(18026937476788898691)
XLA Ops:
  0.0 0.0 copy-start
  0.0 0.7 copy-done
  0.7 0.0 copy-start.1
  0.7 0.7 copy-done.1
  1.3 0.0 copy-start.2
  1.3 0.7 copy-done.2
  2.0 169.9 %shard_map.46 = f32[1024,2048]{1,0:T(8,128)S(1)} custom-call(bf16[1024,2048]{1,0:T(8,128)(2,1)} %bitcast.3, f32[1,4]{1,0:T(1,128)S(1)} %copy-done.1, f32[1,256]{1,0:T(1,128)S(1)} %copy-done, s32[1,2]{1,0:T(1,128)S(1)} %copy-done.2), custom_call_target="tpu_custom_call" | custom-call | flops 34359738368 | bytes 12582912 | tf_op jit(solution)/shard_map/pallas_call | solution.py:287
  171.9 3.4 %copy.6 = f32[1,1024,2048]{2,1,0:T(8,128)} copy(f32[1,1024,2048]{2,1,0:T(8,128)S(1)} %bitcast.2) | data formatting | bytes 16777216
Async XLA Ops:
  0.0 0.7 copy-start
  0.7 0.7 copy-start.1
  1.3 0.7 copy-start.2

commit v3 on v2

v3 whole, which is shorter than its diff:
```python
import functools

import jax
import jax.numpy as jnp
from jax import lax
from jax.experimental import pallas as pl
from jax.experimental.pallas import tpu as pltpu
from jax.sharding import PartitionSpec as P

MESH = pl.DeviceIdType.MESH
RING = 4
PARTS = 32
HALF = PARTS // 2
STEP = PARTS // 4
TICKS = 3 * HALF
AHEAD = 3
STEPS = 16
LEFT, RIGHT, FAR, CROSS, WRAP, RELAY, CHUNKS = (i * HALF for i in (0, 2, 4, 6, 8, 9, 10))
TURN = 8
TO_RIGHT, TO_LEFT, TO_CROSS, TO_WRAP = 0, TURN, 2 * TURN, 2 * TURN + 2 * HALF
TO_RELAY, SENDS = TO_WRAP + HALF, TO_WRAP + 2 * HALF

NT = (((1,), (1,)), ((), ()))


def kernel(
    n, ints_ref, occ_in, vir_in, par_in, gamma,
    occ_ref, vir_ref, par_ref, own, nb, pbuf, xsend, xrecv, abuf, levcol, meta_own, meta_nb,
    send_sem, recv_sem, xs_sem, xr_sem, ms_sem, mr_sem, own_sem, in_sem,
):
    rows, aux = ints_ref.shape
    chunk = rows // PARTS
    step_rows = rows // 4
    virt = vir_ref.shape[1]
    me = lax.axis_index("occ")
    core = lax.axis_index("aux")
    x = me % RING
    right = me - x + (x + 1) % RING
    left = me - x + (x + RING - 1) % RING
    ymain = (me + n + RING - 2 * RING * (x // 2)) % n
    yback = (me + n - RING + 2 * RING * (x // 2)) % n
    near = ((me + 1) % n, (me + n - 1) % n, (me + 2) % n, (me + n - 2) % n)
    edge = (x == 0) | (x == RING - 1)

    first = 1 - (x + 3) // 4
    last = (x + 1) // 4

    def after(k):
        return (me + n - k) // n

    def before(k):
        return (2 * n - 1 - k - me) // n

    has_main = (1 - x // 2) * before(RING) + (x // 2) * after(RING)
    has_back = (1 - x // 2) * after(RING) + (x // 2) * before(RING)
    has_near = (before(1), after(1), before(2), after(2))
    edge_main = edge & (has_main == 1)
    edge_back = edge & (has_back == 1)

    def own_chunk(i):
        return ints_ref.at[pl.ds(pl.multiple_of(i * chunk, chunk), chunk)]

    def nb_chunk(i):
        return nb.at[pl.ds(pl.multiple_of(i * chunk, chunk), chunk)]

    def copy(src, to, ssem, device):
        return pltpu.make_async_remote_copy(
            src_ref=src, dst_ref=nb_chunk(to), send_sem=send_sem.at[ssem], recv_sem=recv_sem.at[to],
            device_id=(device, core), device_id_type=MESH,
        )

    def arrive(i):
        copy(nb_chunk(i), i, 0, right).wait_recv()

    def meta_copy(k, device):
        return pltpu.make_async_remote_copy(
            src_ref=meta_own, dst_ref=meta_nb.at[k], send_sem=ms_sem.at[k], recv_sem=mr_sem.at[k],
            device_id=(device, core), device_id_type=MESH,
        )

    def exchange(s):
        return pltpu.make_async_remote_copy(
            src_ref=xsend.at[s % 2], dst_ref=xrecv.at[s], send_sem=xs_sem.at[s], recv_sem=xr_sem.at[s],
            device_id=(me, 1 - core), device_id_type=MESH,
        )

    load = pltpu.make_async_copy(ints_ref, own, own_sem)
    load.start()
    small = [
        pltpu.make_async_copy(src, dst, in_sem.at[i])
        for i, (src, dst) in enumerate(((occ_in, occ_ref), (vir_in, vir_ref), (par_in, par_ref)))
    ]
    for item in small:
        item.start()

    barrier = pltpu.get_barrier_semaphore()
    def greet(device, other):
        pl.semaphore_signal(barrier, inc=1, device_id=(device, other), device_id_type=MESH)

    greet(right, core)
    greet(left, core)
    greet(me, 1 - core)
    for device, there in zip((ymain, yback, *near), (has_main, has_back, *has_near)):
        pl.when(there == 1)(functools.partial(greet, device, core))
    pl.semaphore_wait(barrier, 3 + has_main + has_back + sum(has_near))

    alternate = 2 * HALF - 3

    def on_own(k, act):
        @pl.when(k < 3)
        def _():
            act(k)

        @pl.when((k >= 3) & (k < alternate) & (k % 2 == 0))
        def _():
            act((k + 2) // 2)

    def on_passed(k, act, end=2 * HALF):
        @pl.when((k >= 3) & (k < alternate) & (k % 2 == 1))
        def _():
            act((k - 3) // 2)

        @pl.when((k >= alternate) & (k < end))
        def _():
            act(k - HALF)

    def send_on_ring(k):
        turn = k % TURN

        def own_first(i):
            copy(own_chunk(i), LEFT + i, TO_RIGHT + turn, right).start()
            copy(own_chunk(HALF + i), RIGHT + HALF + i, TO_LEFT + turn, left).start()

        def passed(i):
            copy(nb_chunk(LEFT + i), FAR + i, TO_RIGHT + turn, right).start()
            copy(nb_chunk(RIGHT + HALF + i), FAR + HALF + i, TO_LEFT + turn, left).start()

        on_own(k, own_first)
        on_passed(k, passed)

        @pl.when((k >= 2 * HALF) & (k < TICKS))
        def _():
            i = k - 2 * HALF

            @pl.when(x < RING - 1)
            def _():
                copy(own_chunk(HALF + i), LEFT + HALF + i, TO_RIGHT + turn, right).start()

            @pl.when(x > 0)
            def _():
                copy(own_chunk(i), RIGHT + i, TO_LEFT + turn, left).start()

            @pl.when(edge_main)
            def _():
                arrive(RELAY + i)

            @pl.when((x == RING - 1) & (has_main == 1))
            def _():
                copy(nb_chunk(RELAY + i), LEFT + HALF + i, TO_RIGHT + turn, right).start()

            @pl.when((x == 0) & (has_main == 1))
            def _():
                copy(nb_chunk(RELAY + i), RIGHT + i, TO_LEFT + turn, left).start()

    pl.loop(0, AHEAD)(send_on_ring)

    @pl.when(edge_back)
    def _():
        @pl.loop(0, HALF)
        def _(i):
            copy(own_chunk(HALF * (x // 2) + i), RELAY + i, TO_RELAY + i, yback).start()

    for item in small:
        item.wait()
    for i in range(rows // virt):
        meta_own[0:1, i * virt : (i + 1) * virt] = vir_ref[...] - occ_ref[0:1, i : i + 1]
    for reach in (1, 2):
        found = [jnp.where(par_ref[0:1, i : i + 1] == me + reach, 1.0, 0.0) for i in range(2)]
        meta_own[reach : reach + 1, :] = jnp.broadcast_to(jnp.maximum(*found), (1, rows))
    meta_own[3:8, :] = jnp.zeros((5, rows), jnp.float32)
    for k, device in enumerate(near):
        pl.when(has_near[k] == 1)(meta_copy(k, device).start)
    levcol[...] = jnp.broadcast_to(meta_own[0:1, :], (levcol.shape[1], rows)).T

    @pl.loop(0, 4)
    def _(i):
        here = pl.ds(pl.multiple_of(i * step_rows, step_rows), step_rows)
        gamma[here] = jnp.zeros((step_rows, aux), jnp.float32)

    has_slot = (after(1), before(1), after(2), before(2))
    for k in range(4):

        @pl.when(has_slot[k] == 1)
        def _():
            meta_copy(k, right).wait_recv()
            listed = 1 + k // 2
            meta_nb[k, 3:4, :] = meta_own[listed : listed + 1, :] if k % 2 else meta_nb[k, listed : listed + 1, :]

    load.wait()

    def send_across(j):
        group = j // STEP
        i = HALF * (group % 2) + STEP * (group // 2) + j % STEP

        @pl.when(has_main == 1)
        def _():
            copy(nb_chunk(FAR + i), CROSS + i, TO_CROSS + j, ymain).start()

    def links(t):
        def own_first(i):
            arrive(LEFT + i)
            arrive(RIGHT + HALF + i)

            @pl.when(edge_main)
            def _():
                copy(nb_chunk((RIGHT + HALF) // 3 * x + i), WRAP + i, TO_WRAP + i, ymain).start()

        def passed(i):
            arrive(FAR + i)
            arrive(FAR + HALF + i)

        relayed = t // (2 * HALF)

        @pl.when((1 - has_main) * relayed * last == 0)
        def _():
            copy(nb_chunk(0), 0, TO_RIGHT + t % TURN, right).wait_send()

        @pl.when((1 - has_main) * relayed * first == 0)
        def _():
            copy(nb_chunk(0), 0, TO_LEFT + t % TURN, left).wait_send()

        on_own(t, own_first)
        on_passed(t, passed)
        send_on_ring(t + AHEAD)
        on_passed(t, send_across, TICKS)


    def ticks_before(s):
        return 7 + s + (s + 14) // 16 + 2 * ((s + 11) // 16)

    def place(s):
        late = (s + 6) // 16
        early = 1 - late
        p = early * (s // 5) + late * ((s - 10) // 3)
        r = early * (s % 5) + late * (2 * ((s - 10) % 3))
        across = r // 4
        r2 = (r // 2) * (1 - across)
        h = r % 2
        base = (1 - across) * (1 - r2)
        swap = early * base * ((1 - h) * first + h * last)
        group = p + 2 * late
        at = (
            early * base * (1 - swap) * h * (RIGHT + HALF)
            + swap * WRAP
            + early * r2 * (FAR + HALF * h)
            + late * base * (LEFT + HALF)
            + late * r2 * RIGHT
            + (1 - across) * STEP * p
            + across * (CROSS + HALF * (group % 2) + STEP * (group // 2))
        )
        inside = (
            (1 - across) * (HALF * (early * h + late * base) + STEP * p)
            + across * (HALF * (group % 2) + STEP * (group // 2))
        )
        slot = early * (base * h + r2 * (3 - x // 2)) + late * r2 + across * (2 + x // 2)
        waits = swap + across + late * (1 - across)
        foreign = swap + across + late * (base * first + r2 * last)
        return at, inside, slot, waits, 1 - foreign * (1 - has_back)

    def block_rows(at):
        return pl.ds(pl.multiple_of(at * chunk, chunk), step_rows)

    m_rows = rows // 2
    n_cols = aux // 4

    def sent(s):
        @pl.when(place(s)[4] == 1)
        def _():
            exchange(s).wait_send()

    def products(s):
        at, _, _, waits, _ = place(s)

        @pl.when(waits == 1)
        def _():
            pl.loop(0, STEP)(lambda i: arrive(at + i))

        @pl.loop(0, rows // m_rows)
        def _(m):
            here = pl.ds(pl.multiple_of(m * m_rows, m_rows), m_rows)
            part = lax.dot_general(own[here], nb[block_rows(at)], NT, preferred_element_type=jnp.float32)
            pbuf[s % 2, here] = part
            xsend[s % 2, here] = part.astype(jnp.bfloat16)

        exchange(s).start()

    def finish(s):
        at, inside, slot, _, _ = place(s)
        exchange(s).wait_recv()
        cols = pl.ds(pl.multiple_of(inside * chunk, step_rows), step_rows)
        level = meta_nb[slot, 0:1, cols]
        live = meta_nb[slot, 3:4, cols]
        wide = step_rows // levcol.shape[1]

        @pl.loop(0, 4)
        def _(m):
            here = pl.ds(pl.multiple_of(m * step_rows, step_rows), step_rows)
            total = pbuf[s % 2, here] + xrecv[s, here].astype(jnp.float32)
            mine = levcol[here]
            mine = jnp.concatenate([mine] * wide, axis=1)
            abuf[here] = jnp.where(live > 0.5, total / (mine + level), 0.0).astype(jnp.bfloat16)

        @pl.loop(0, aux // n_cols)
        def _(c):
            there = pl.ds(pl.multiple_of(c * n_cols, n_cols), n_cols)
            gamma[:, there] += jnp.dot(abuf[...], nb[block_rows(at), there], preferred_element_type=jnp.float32)

    fine = PARTS // 16

    def links_until(start, end):
        @pl.loop(start, end)
        def _(t):
            @pl.when(t < TICKS)
            def _():
                links(t)

    links_until(0, fine * ticks_before(0))

    @pl.loop(0, STEPS + 2)
    def _(s):
        now = fine * ticks_before(s)
        made = s - (s + 2) // 16
        ended = s - 1 - (s + 1) // 16

        @pl.when((s != 13) & (made >= 2) & (made < STEPS))
        def _():
            sent(made - 2)

        @pl.when((s != 13) & (made < STEPS))
        def _():
            pl.when(place(made)[4] == 1)(functools.partial(products, made))

        links_until(now, now + 1)

        @pl.when((s != 14) & (ended >= 0))
        def _():
            pl.when(place(ended)[4] == 1)(functools.partial(finish, ended))

        links_until(now + 1, fine * ticks_before(s + 1))

    def sent_all(start, end):
        @pl.loop(start, end)
        def _(k):
            copy(nb_chunk(0), 0, k, right).wait_send()

    pl.when(has_main == 1)(functools.partial(sent_all, TO_CROSS, TO_WRAP))
    pl.when(edge_main)(functools.partial(sent_all, TO_WRAP, TO_RELAY))
    pl.when(edge_back)(functools.partial(sent_all, TO_RELAY, SENDS))
    for k in range(4):
        pl.when(has_near[k] == 1)(meta_copy(k, right).wait_send)
    sent(STEPS - 2)
    sent(STEPS - 1)


def body(n, ints, occ_energy, vir_energy, partners):
    _, rows, aux = ints.shape
    lanes = min(128, rows // 4)
    step_rows = rows // 4
    result = pl.pallas_call(
        functools.partial(kernel, n),
        out_shape=pltpu.VMEM((rows, aux), jnp.float32),
        in_specs=[
            pl.BlockSpec(memory_space=pl.ANY),
            pl.BlockSpec(memory_space=pl.ANY),
            pl.BlockSpec(memory_space=pl.ANY),
            pl.BlockSpec(memory_space=pl.ANY),
        ],
        out_specs=pl.BlockSpec(memory_space=pltpu.VMEM),
        scratch_shapes=[
            pltpu.VMEM(occ_energy.shape, jnp.float32),
            pltpu.VMEM(vir_energy.shape, jnp.float32),
            pltpu.VMEM(partners.shape, jnp.int32),
            pltpu.VMEM((rows, aux), jnp.bfloat16),
            pltpu.VMEM((CHUNKS * rows // PARTS, aux), jnp.bfloat16),
            pltpu.VMEM((2, rows, step_rows), jnp.float32),
            pltpu.VMEM((2, rows, step_rows), jnp.bfloat16),
            pltpu.VMEM((STEPS, rows, step_rows), jnp.bfloat16),
            pltpu.VMEM((rows, step_rows), jnp.bfloat16),
            pltpu.VMEM((rows, lanes), jnp.float32),
            pltpu.VMEM((8, rows), jnp.float32),
            pltpu.VMEM((4, 8, rows), jnp.float32),
            pltpu.SemaphoreType.DMA((SENDS,)),
            pltpu.SemaphoreType.DMA((CHUNKS,)),
            pltpu.SemaphoreType.DMA((STEPS,)),
            pltpu.SemaphoreType.DMA((STEPS,)),
            pltpu.SemaphoreType.DMA((4,)),
            pltpu.SemaphoreType.DMA((4,)),
            pltpu.SemaphoreType.DMA,
            pltpu.SemaphoreType.DMA((3,)),
        ],
        compiler_params=pltpu.CompilerParams(
            collective_id=0, has_side_effects=True, vmem_limit_bytes=55 * 2**20
        ),
        cost_estimate=pl.CostEstimate(
            flops=16 * rows * rows * aux, bytes_accessed=6 * rows * aux, transcendentals=0
        ),
    )(ints[0], occ_energy, vir_energy, partners)
    return result[None]


def solution(mesh):
    return jax.shard_map(
        functools.partial(body, mesh.shape["occ"]),
        mesh=mesh,
        in_specs=(P("occ", None, "aux"), P("occ", None), P("occ", None), P("occ", None)),
        out_specs=P("occ", None, "aux"),
        check_vma=False,
    )
```

time: 175 us -> 166 us (0.949)
  the two profiles are of different devices: /device:TPU:1 before, /device:TPU:32 now
where the time goes in v3:
time: 166 us; the launch traced here: 165 us
  Pallas kernels  162 us (98%)
  local copies, waits for them, and re-layouts  3.4 us (2%)
    pallas_call x1, Pallas kernels, body(): pl.pallas_call(functools.partial(kernel, n), out_shape=pltpu.VMEM((rows,...  162 us
    unnamed x1, local copies, waits for them, and re-layouts  3.4 us

profile of v3, /device:TPU:32, one launch (start us, length us, event | category | flops | bytes accessed | tf_op | source)
XLA Modules:
  0.0 165.4 jit_solution(17163883015163282386)
XLA Ops:
  0.0 162.0 %shard_map.46 = f32[1024,2048]{1,0:T(8,128)S(1)} custom-call(bf16[1024,2048]{1,0:T(8,128)(2,1)} %bitcast.3, f32[1,4]{1,0:T(1,128)} %occ_in.1, f32[1,256]{1,0:T(1,128)} %vir_in.1, s32[1,2]{1,0:T(1,128)} %par_in.1), custom_call_target="tpu_custom_call" | custom-call | flops 34359738368 | bytes 12582912 | tf_op jit(solution)/shard_map/pallas_call | solution.py:369
  162.0 3.4 %copy.6 = f32[1,1024,2048]{2,1,0:T(8,128)} copy(f32[1,1024,2048]{2,1,0:T(8,128)S(1)} %bitcast.2) | data formatting | bytes 16777216

commit v4 on v3

--- a/solution.py
+++ b/solution.py
@@ -14,6 +14,8 @@
 STEP = PARTS // 4
 TICKS = 3 * HALF
 AHEAD = 3
+EARLY = 8
+LATE = 0
 STEPS = 16
 LEFT, RIGHT, FAR, CROSS, WRAP, RELAY, CHUNKS = (i * HALF for i in (0, 2, 4, 6, 8, 9, 10))
 TURN = 8
@@ -115,12 +117,12 @@
         def _():
             act((k + 2) // 2)
 
-    def on_passed(k, act, end=2 * HALF):
+    def on_passed(k, act):
         @pl.when((k >= 3) & (k < alternate) & (k % 2 == 1))
         def _():
             act((k - 3) // 2)
 
-        @pl.when((k >= alternate) & (k < end))
+        @pl.when((k >= alternate) & (k < 2 * HALF))
         def _():
             act(k - HALF)
 
@@ -206,6 +208,17 @@
         def _():
             copy(nb_chunk(FAR + i), CROSS + i, TO_CROSS + j, ymain).start()
 
+    def send_on_across(t):
+        on_passed(t, send_across)
+
+        @pl.when(t == 2 * HALF)
+        def _():
+            pl.loop(HALF, HALF + EARLY)(send_across)
+
+        @pl.when((t >= 2 * HALF) & (t < TICKS - EARLY))
+        def _():
+            send_across(t - HALF + EARLY)
+
     def links(t):
         def own_first(i):
             arrive(LEFT + i)
@@ -221,22 +234,27 @@
 
         relayed = t // (2 * HALF)
 
-        @pl.when((1 - has_main) * relayed * last == 0)
+        @pl.when((t < TICKS) & ((1 - has_main) * relayed * last == 0))
         def _():
             copy(nb_chunk(0), 0, TO_RIGHT + t % TURN, right).wait_send()
 
-        @pl.when((1 - has_main) * relayed * first == 0)
+        @pl.when((t < TICKS) & ((1 - has_main) * relayed * first == 0))
         def _():
             copy(nb_chunk(0), 0, TO_LEFT + t % TURN, left).wait_send()
 
-        on_own(t, own_first)
-        on_passed(t, passed)
+        @pl.when(t >= LATE)
+        def _():
+            on_own(t - LATE, own_first)
+            on_passed(t - LATE, passed)
+
         send_on_ring(t + AHEAD)
-        on_passed(t, send_across, TICKS)
-
+
+        @pl.when(t >= LATE)
+        def _():
+            send_on_across(t - LATE)
 
     def ticks_before(s):
-        return 7 + s + (s + 14) // 16 + 2 * ((s + 11) // 16)
+        return 8 + s + 3 * ((s + 11) // 16)
 
     def place(s):
         late = (s + 6) // 16
@@ -270,8 +288,8 @@
     def block_rows(at):
         return pl.ds(pl.multiple_of(at * chunk, chunk), step_rows)
 
-    m_rows = rows // 2
-    n_cols = aux // 4
+    m_rows = rows
+    n_cols = aux
 
     def sent(s):
         @pl.when(place(s)[4] == 1)
@@ -320,7 +338,7 @@
     def links_until(start, end):
         @pl.loop(start, end)
         def _(t):
-            @pl.when(t < TICKS)
+            @pl.when(t < TICKS + LATE)
             def _():
                 links(t)
 

time: 166 us -> 165 us (level)
  no operation moved by 1% of the time
where the time goes in v4:
time: 165 us; the launch traced here: 164 us
  Pallas kernels  161 us (98%)
  local copies, waits for them, and re-layouts  3.4 us (2%)
    pallas_call x1, Pallas kernels, body(): pl.pallas_call(functools.partial(kernel, n), out_shape=pltpu.VMEM((rows,...  161 us
    unnamed x1, local copies, waits for them, and re-layouts  3.4 us

profile of v4, /device:TPU:32, one launch (start us, length us, event | category | flops | bytes accessed | tf_op | source)
XLA Modules:
  0.0 164.2 jit_solution(7663229502585079681)
XLA Ops:
  0.0 160.8 %shard_map.46 = f32[1024,2048]{1,0:T(8,128)S(1)} custom-call(bf16[1024,2048]{1,0:T(8,128)(2,1)} %bitcast.3, f32[1,4]{1,0:T(1,128)} %occ_in.1, f32[1,256]{1,0:T(1,128)} %vir_in.1, s32[1,2]{1,0:T(1,128)} %par_in.1), custom_call_target="tpu_custom_call" | custom-call | flops 34359738368 | bytes 12582912 | tf_op jit(solution)/shard_map/pallas_call | solution.py:387
  160.8 3.4 %copy.6 = f32[1,1024,2048]{2,1,0:T(8,128)} copy(f32[1,1024,2048]{2,1,0:T(8,128)S(1)} %bitcast.2) | data formatting | bytes 16777216

commit v5 on v4

--- a/solution.py
+++ b/solution.py
@@ -13,9 +13,9 @@
 HALF = PARTS // 2
 STEP = PARTS // 4
 TICKS = 3 * HALF
-AHEAD = 3
+AHEAD = 2
 EARLY = 8
-LATE = 0
+LATE = 1
 STEPS = 16
 LEFT, RIGHT, FAR, CROSS, WRAP, RELAY, CHUNKS = (i * HALF for i in (0, 2, 4, 6, 8, 9, 10))
 TURN = 8
@@ -320,9 +320,9 @@
         live = meta_nb[slot, 3:4, cols]
         wide = step_rows // levcol.shape[1]
 
-        @pl.loop(0, 4)
+        @pl.loop(0, 1)
         def _(m):
-            here = pl.ds(pl.multiple_of(m * step_rows, step_rows), step_rows)
+            here = pl.ds(pl.multiple_of(m * rows, rows), rows)
             total = pbuf[s % 2, here] + xrecv[s, here].astype(jnp.float32)
             mine = levcol[here]
             mine = jnp.concatenate([mine] * wide, axis=1)

time: 165 us -> 164 us (level)
  no operation moved by 1% of the time
where the time goes in v5:
time: 164 us; the launch traced here: 163 us
  Pallas kernels  160 us (98%)
  local copies, waits for them, and re-layouts  3.4 us (2%)
    pallas_call x1, Pallas kernels, body(): pl.pallas_call(functools.partial(kernel, n), out_shape=pltpu.VMEM((rows,...  160 us
    unnamed x1, local copies, waits for them, and re-layouts  3.4 us

profile of v5, /device:TPU:32, one launch (start us, length us, event | category | flops | bytes accessed | tf_op | source)
XLA Modules:
  0.0 163.4 jit_solution(16590240779447115428)
XLA Ops:
  0.0 160.0 %shard_map.46 = f32[1024,2048]{1,0:T(8,128)S(1)} custom-call(bf16[1024,2048]{1,0:T(8,128)(2,1)} %bitcast.3, f32[1,4]{1,0:T(1,128)} %occ_in.1, f32[1,256]{1,0:T(1,128)} %vir_in.1, s32[1,2]{1,0:T(1,128)} %par_in.1), custom_call_target="tpu_custom_call" | custom-call | flops 34359738368 | bytes 12582912 | tf_op jit(solution)/shard_map/pallas_call | solution.py:387
  160.0 3.4 %copy.6 = f32[1,1024,2048]{2,1,0:T(8,128)} copy(f32[1,1024,2048]{2,1,0:T(8,128)S(1)} %bitcast.2) | data formatting | bytes 16777216

commit v6 on v5

--- a/solution.py
+++ b/solution.py
@@ -14,7 +14,7 @@
 STEP = PARTS // 4
 TICKS = 3 * HALF
 AHEAD = 2
-EARLY = 8
+EARLY = 12
 LATE = 1
 STEPS = 16
 LEFT, RIGHT, FAR, CROSS, WRAP, RELAY, CHUNKS = (i * HALF for i in (0, 2, 4, 6, 8, 9, 10))

time: 164 us -> 164 us (level)
  no operation moved by 1% of the time
where the time goes in v6:
time: 164 us; the launch traced here: 163 us
  Pallas kernels  160 us (98%)
  local copies, waits for them, and re-layouts  3.4 us (2%)
    pallas_call x1, Pallas kernels, body(): pl.pallas_call(functools.partial(kernel, n), out_shape=pltpu.VMEM((rows,...  160 us
    unnamed x1, local copies, waits for them, and re-layouts  3.4 us

profile of v6, /device:TPU:32, one launch (start us, length us, event | category | flops | bytes accessed | tf_op | source)
XLA Modules:
  0.0 163.4 jit_solution(4629367085203145601)
XLA Ops:
  0.0 160.0 %shard_map.46 = f32[1024,2048]{1,0:T(8,128)S(1)} custom-call(bf16[1024,2048]{1,0:T(8,128)(2,1)} %bitcast.3, f32[1,4]{1,0:T(1,128)} %occ_in.1, f32[1,256]{1,0:T(1,128)} %vir_in.1, s32[1,2]{1,0:T(1,128)} %par_in.1), custom_call_target="tpu_custom_call" | custom-call | flops 34359738368 | bytes 12582912 | tf_op jit(solution)/shard_map/pallas_call | solution.py:387
  160.0 3.4 %copy.6 = f32[1,1024,2048]{2,1,0:T(8,128)} copy(f32[1,1024,2048]{2,1,0:T(8,128)S(1)} %bitcast.2) | data formatting | bytes 16777216
